TPU v7x, 512 devices: a whole 4x8x8 slice. The times are simulated.
512 devices in a mesh: blk: 128 (over y, z, core), pair: 4 (over x).
Axes of the slice: x: 4, y: 8, z: 8, core: 2. Of those that a mesh axis runs over, the one named last changes fastest.
Arguments:
- raw: bfloat16 [128, 128, 16384], P('blk', 'pair'), may hold values from -6 to 6
- pair_list: int32 [768, 2], replicated, may hold values from 0 to 127, as said below
Outputs:
- stack: float32 [128, 128, 16, 512], P('blk', 'pair')
Inputs may be any that keep to these rules, and one draw needn't show every extreme that they name: `pair_list`: each row (i, j) names two blocks with 1 <= j - i <= 8 and j < 128; no pair appears twice.
All inputs are finite; a program needn't handle non-finite values.
Results may differ from a plain program's by a relative error of at most 0.0062.
Values may be sent and summed in bfloat16 or wider, within the bound.
A program may use at most 64 MiB of HBM per device.

v0:
```python
import math

import jax
import jax.numpy as jnp
import ml_dtypes
import numpy as np
from jax import lax
from jax.experimental import pallas as pl
from jax.experimental.pallas import tpu as pltpu
from jax.sharding import PartitionSpec as P

SPLIT = 128
NT = SPLIT * SPLIT
NBAND = 20
REACH = 8
LAG = 512
ROW = 16
NROW = 8
PAIR = 4
HALF = SPLIT // 2
BINS = 2 * NBAND
NBINS = HALF * BINS
EPSILON = 1e-06
VMEM = 56 * 1024 * 1024
MESH = pl.DeviceIdType.MESH
bf16 = jnp.bfloat16
f32 = jnp.float32


def first_table():
    angle = 2.0 * np.pi / SPLIT * (np.outer(np.arange(SPLIT), np.arange(SPLIT)) % SPLIT)
    table = np.concatenate([np.cos(angle[: HALF + 1]), -np.sin(angle[1:HALF])])
    return table.astype(ml_dtypes.bfloat16)


def slot_bins():
    slot = np.arange(HALF)[:, None, None]
    band = np.arange(NBAND)[None, :, None]
    mirror = np.where(slot == 0, HALF, SPLIT - slot)
    low = np.where(np.arange(2)[None, None, :] == 0, slot, mirror)
    return (low + SPLIT * band).reshape(HALF, BINS)


def angle_of(product):
    return 2.0 * np.pi / NT * (product % NT)


def second_tables():
    bins = slot_bins()
    worker, h = np.arange(PAIR)[:, None], np.arange(8)[None, :]
    sample = (32 * worker + h).reshape(-1)
    phi = angle_of(bins[:, :, None] * sample)
    cos, sin = np.cos(phi), np.sin(phi)
    sign = np.where(np.arange(BINS) % 2 == 0, 1.0, -1.0)[None, :, None]
    re = np.concatenate([cos, sign * sin], 2)
    im = np.concatenate([-sin, sign * cos], 2)
    zero = np.zeros_like(cos[0])
    even = (np.arange(BINS) % 2 == 0)[:, None]
    re[0] = np.concatenate([np.where(even, cos[0], zero), np.where(even, zero, cos[0])], 1)
    im[0] = np.concatenate([np.where(even, -sin[0], zero), np.where(even, zero, -sin[0])], 1)
    full = np.concatenate([re, im], 1)
    high = full.astype(ml_dtypes.bfloat16)
    low = (full - high.astype(np.float64)).astype(ml_dtypes.bfloat16)
    weights = np.concatenate([high, high, low], 2)
    quarter = np.repeat(8 * np.arange(4), 32)
    psi = angle_of(bins[:, :, None] * quarter)
    return weights, np.cos(psi).astype(np.float32), np.sin(psi).astype(np.float32)


def lag_tables():
    angle = angle_of(np.arange(LAG)[:, None] * slot_bins().reshape(-1)[None, :])
    return np.cos(angle).astype(ml_dtypes.bfloat16), np.sin(angle).astype(ml_dtypes.bfloat16)


def order_tables():
    near = np.zeros((256, 256), ml_dtypes.bfloat16)
    far = np.zeros((256, 256), ml_dtypes.bfloat16)
    for block in range(ROW):
        for e in range(2):
            for d in range(REACH):
                row = block * 16 + e * 8 + d
                near[row, 32 * d + 2 * block + e] = 1
                far[row, 32 * d + 2 * ((block - d - 1) % ROW) + e] = 1
    return np.stack([near, far])


def ahead_table():
    table = np.zeros((8, 256, 256), ml_dtypes.bfloat16)
    for g in range(8):
        for column in range(256):
            c = column % 32 + 2 * (column // 32 + 1)
            table[g, c if c < 32 else 128 + 16 * g + c - 32, column] = 1
    return table


def swap_bits(tiles, bits):
    lane = lax.broadcasted_iota(jnp.int32, tiles[0].shape, 1)
    tiles = list(tiles)
    for bit, shift in bits:
        low_half = (lane & shift) == 0
        for low in range(len(tiles)):
            if low & bit:
                continue
            a, b = tiles[low], tiles[low | bit]
            tiles[low] = jnp.where(low_half, a, pltpu.roll(b, shift, 1))
            tiles[low | bit] = jnp.where(low_half, pltpu.roll(a, 128 - shift, 1), b)
    return tiles


WAVES = ((3, 5), (0, 4), (2, 6), (1, 7))
CHUNKS = 4
CROWS = NBINS // CHUNKS
EROWS = CROWS // 8
TCH = 2
TW = LAG // TCH


def whole_kernel(
    raw_hbm, pair_ref, t_hbm, w_hbm, c_hbm, s_hbm, lc_hbm, ls_hbm, order_hbm, ahead_hbm, out_ref,
    raw_ref, t_ref, w_ref, c_ref, s_ref, lc_ref, ls_ref, order_ref, ahead_ref,
    sent, landed, quarters, zs, wide, first, spec_re, spec_im, white, edge_out, edge_in,
    cross_re, cross_im, near_out, wrap_out, wrap_in, far_out, near_in, far_in,
    load_sem, a_send, a_recv, x_send, x_recv, e_send, e_recv, n_send, n_recv, f_send, f_recv, w_send, w_recv,
):
    me, worker = lax.axis_index("blk"), lax.axis_index("pair")
    row, place = me // ROW, me % ROW
    behind = lax.rem(row + NROW - 1, NROW) * ROW + place
    ahead = lax.rem(row + 1, NROW) * ROW + place

    loads = [
        pltpu.make_async_copy(source, target, load_sem.at[k])
        for k, (source, target) in enumerate(
            (
                (raw_hbm, raw_ref), (t_hbm, t_ref), (w_hbm, w_ref), (c_hbm, c_ref), (s_hbm, s_ref),
                (ahead_hbm, ahead_ref), (lc_hbm, lc_ref), (ls_hbm, ls_ref), (order_hbm, order_ref),
            )
        )
    ]
    for load in loads:
        load.start()

    def remote(source, target, send, recv, blk, pair):
        return pltpu.make_async_remote_copy(
            src_ref=source, dst_ref=target, send_sem=send, recv_sem=recv, device_id=(blk, pair), device_id_type=MESH
        )

    barrier = pltpu.get_barrier_semaphore()

    def greet(step, carry):
        pl.semaphore_signal(
            barrier, inc=1, device_id=(lax.rem(me + step, SPLIT), worker), device_id_type=MESH
        )
        return carry

    lax.fori_loop(1, SPLIT, greet, 0)
    for step in range(1, PAIR):
        pl.semaphore_signal(
            barrier, inc=1, device_id=(me, lax.rem(worker + step, PAIR)), device_id_type=MESH
        )

    loads[0].wait()

    def spread(index, carry):
        to_row, half = index // 2, index % 2
        rows = pl.ds(pl.multiple_of(half * 16, 16), 16)
        tiles = []
        for block in range(ROW):
            at = pl.multiple_of(to_row * 2048 + block * 128, 128)
            tiles.append(raw_ref[0, rows, pl.ds(at, 128)].astype(f32))
        tiles = swap_bits(tiles, [(1, 2), (2, 4), (4, 8), (8, 16)])
        for block in range(ROW):
            sent[to_row * ROW + block, rows, :] = tiles[block].astype(bf16)
        return carry

    lax.fori_loop(0, 16, spread, 0)

    lane = lax.broadcasted_iota(jnp.int32, (1, 256), 1)
    leading = row * ROW + (lane // 2) % ROW
    trailing = leading + lane // 32 + 1
    listed = pair_ref[...]
    found = (listed[:, 0:1] == leading) & (listed[:, 1:2] == trailing)
    present = jnp.max(jnp.where(found, 1.0, 0.0), axis=0, keepdims=True)

    pl.semaphore_wait(barrier, SPLIT - 1 + PAIR - 1)

    for wave, (one, two) in enumerate(WAVES):

        def send(step, carry, wave=wave, one=one, two=two):
            to_row = lax.rem(row + one + (two - one) * (step % 2), NROW)
            shift = ((step // 2) * 7) % 16
            chip = lax.rem(place // 2 + shift // 2, 8)
            there = to_row * ROW + chip * 2 + lax.rem(place % 2 + shift % 2, 2)
            remote(sent.at[there], landed.at[me], a_send, a_recv.at[wave], there, worker).start()
            return carry

        lax.fori_loop(1 if one == 0 else 0, 32, send, 0)
    landed[me] = sent[me]

    for wave, (one, two) in enumerate(WAVES):
        count = 31 if one == 0 else 32
        remote(
            sent.at[pl.ds(0, count)], landed.at[pl.ds(0, count)], a_send, a_recv.at[wave], ahead, worker
        ).wait_recv()
        for distance in (one, two):
            from_row = lax.rem(row + NROW - distance, NROW)

            def quarter(index, carry, from_row=from_row):
                parts = []
                for k in range(2):
                    block = landed[from_row * ROW + index * 2 + k].astype(f32)
                    tiles = [block[8 * q : 8 * q + 8] for q in range(4)]
                    parts.append(swap_bits(tiles, [(1, 32), (2, 64)]))
                at = pl.ds(pl.multiple_of(from_row * 128 + index * 16, 16), 16)
                for w in range(PAIR):
                    quarters[w, at, :] = jnp.concatenate([parts[0][w], parts[1][w]], 0).astype(bf16)
                return carry

            lax.fori_loop(0, 8, quarter, 0, unroll=4)
            at = pl.ds(pl.multiple_of(from_row * 128, 128), 128)
            for step in range(1, PAIR):
                there = lax.rem(worker + step, PAIR)
                remote(
                    quarters.at[there, at], zs.at[worker, at], x_send, x_recv.at[wave], me, there
                ).start()
            zs[worker, at, :] = quarters[worker, at, :]

    for load in loads[1:]:
        load.wait()
    for wave, (one, two) in enumerate(WAVES):
        part = zs.at[pl.ds(0, PAIR - 1), pl.ds(0, 256)]
        remote(part, part, x_send, x_recv.at[wave], me, lax.rem(worker + 1, PAIR)).wait_recv()
        for distance in (one, two):
            from_row = lax.rem(row + NROW - distance, NROW)
            at = pl.multiple_of(from_row * 128, 128)
            for w in range(PAIR):
                wide[pl.ds(1024 * w + at, 128), :] = zs[w, pl.ds(at, 128), :].astype(f32)
    table = t_ref[...]

    def transform(index, carry):
        at = (index // 4) * 1024 + (index % 4) * 2
        pair = [wide[pl.ds(at + k, 128, stride=8), :].astype(bf16) for k in range(2)]
        got = jnp.dot(table, jnp.concatenate(pair, 1), preferred_element_type=f32)
        first[index * 2] = got[:, :128]
        first[index * 2 + 1] = got[:, 128:]
        return carry

    lax.fori_loop(0, 16, transform, 0, unroll=8)
    flat = first.reshape(32 * 128, 128)

    def bands(slot, power):
        a = flat[pl.ds(slot, 32, stride=128), :]
        b = flat[pl.ds(slot + HALF, 32, stride=128), :]
        both = jnp.concatenate([a, b], 0)
        high = both.astype(bf16)
        low = (both - high.astype(f32)).astype(bf16)
        got = jnp.dot(
            w_ref[slot], jnp.concatenate([high, low, high], 0), preferred_element_type=f32
        )
        part_re, part_im = got[:BINS], got[BINS:]
        cos, sin = c_ref[slot], s_ref[slot]
        re = part_re * cos + part_im * sin
        im = part_im * cos - part_re * sin
        re = re + pltpu.roll(re, 64, 1)
        im = im + pltpu.roll(im, 64, 1)
        re = re + pltpu.roll(re, 32, 1)
        im = im + pltpu.roll(im, 32, 1)
        at = pl.ds(pl.multiple_of(slot * BINS, 8), BINS)
        spec_re[at, :] = re
        spec_im[at, :] = im
        return power + re * re + im * im

    power = lax.fori_loop(0, HALF, bands, jnp.zeros((BINS, 128), f32), unroll=8)
    parity = lax.broadcasted_iota(jnp.int32, (BINS, 128), 0) % 2
    other = jnp.where(parity == 0, pltpu.roll(power, BINS - 1, 0), pltpu.roll(power, 1, 0))
    gain = lax.rsqrt((power + other) / SPLIT + EPSILON)
    gain = jnp.concatenate([gain, gain], 0)
    group = lax.broadcasted_iota(jnp.int32, (EROWS, 128), 1) // 16

    for chunk in range(CHUNKS):
        for k, spec in enumerate((spec_re, spec_im)):
            packed = None
            for g in range(8):
                at = pl.ds(CROWS * chunk + EROWS * g, EROWS)
                value = (spec[at, :] * gain).astype(bf16)
                white[k, at, :] = value
                value = value.astype(f32)
                value = pltpu.roll(value, 16, 1) if g % 2 else value
                packed = value if g == 0 else jnp.where(group == g, value, packed)
            edge_out[chunk, k] = packed.astype(bf16)
        remote(
            edge_out.at[chunk], edge_in.at[chunk], e_send.at[chunk], e_recv.at[chunk], behind, worker
        ).start()

    for chunk in range(CHUNKS):
        remote(
            edge_out.at[chunk], edge_in.at[chunk], e_send.at[chunk], e_recv.at[chunk], behind, worker
        ).wait()

        def cross(g, carry, chunk=chunk):
            at = pl.ds(pl.multiple_of(CROWS * chunk + EROWS * g, 16), EROWS)
            own = [white[k, at, :] for k in range(2)]
            both = [jnp.concatenate([own[k], edge_in[chunk, k]], 1) for k in range(2)]
            got = jnp.dot(
                jnp.concatenate(both, 0), ahead_ref[g], preferred_element_type=f32
            )
            a, f = own[0].astype(f32), own[1].astype(f32)
            for tile in range(2):
                columns = slice(128 * tile, 128 * tile + 128)
                e, h = got[:EROWS, columns], got[EROWS:, columns]
                cross_re[at, columns] = (a * e + f * h).astype(bf16)
                cross_im[at, columns] = (f * e - a * h).astype(bf16)
            return carry

        lax.fori_loop(0, 8, cross, 0, unroll=2)

    inv_root = 1.0 / math.sqrt(NBINS)
    offset = lax.broadcasted_iota(jnp.int32, (16, TW), 0) % REACH
    nt = (((1,), (1,)), ((), ()))
    for t in range(TCH):
        lags = pl.ds(TW * t, TW)
        even = jnp.dot(lc_ref[lags, :], cross_re[...], preferred_element_type=f32)
        odd = jnp.dot(ls_ref[lags, :], cross_im[...], preferred_element_type=f32)
        near, far = (
            jnp.where(present > 0.5, half * inv_root, 0.0).astype(bf16)
            for half in (even - odd, even + odd)
        )
        far = lax.dot_general(order_ref[1], far, nt, preferred_element_type=f32).astype(bf16)
        wrap_out[t] = far[: 16 * REACH]
        far_out[t] = far
        remote(wrap_out.at[t], wrap_in.at[t], w_send.at[t], w_recv.at[t], ahead, worker).start()
        near = lax.dot_general(order_ref[0], near, nt, preferred_element_type=f32).astype(bf16)
        near_out[t] = near.reshape(ROW, 16, TW)

        def send_near(step, carry, t=t):
            to = lax.rem(place + (step * 7) % 16, ROW)
            remote(
                near_out.at[t, to], near_in.at[t, place], n_send, n_recv.at[t], row * ROW + to, worker
            ).start()
            return carry

        lax.fori_loop(1, ROW, send_near, 0)

    for t in range(TCH):
        remote(wrap_out.at[t], wrap_in.at[t], w_send.at[t], w_recv.at[t], ahead, worker).wait()
        for block in range(REACH):
            at = pl.ds(16 * block, 16)
            far_out[t, at, :] = jnp.where(
                offset < block, far_out[t, at, :].astype(f32), wrap_in[t, at, :].astype(f32)
            ).astype(bf16)

        def send_far(step, carry, t=t):
            to = lax.rem(place + (step * 7) % 16, ROW)
            at = pl.ds(pl.multiple_of(to * 16, 16), 16)
            remote(
                far_out.at[t, at], far_in.at[t, place], f_send, f_recv.at[t], row * ROW + to, worker
            ).start()
            return carry

        lax.fori_loop(1, ROW, send_far, 0)

    for t in range(TCH):
        near_in[t, place] = near_out[t, place]
        far_in[t, place] = far_out[t, pl.ds(pl.multiple_of(place * 16, 16), 16), :]
    for half, (arrived, send, recv) in enumerate(((near_in, n_send, n_recv), (far_in, f_send, f_recv))):
        for t in range(TCH):
            most = arrived.at[t, pl.ds(0, ROW - 1)]
            remote(most, most, send, recv.at[t], ahead, worker).wait_recv()

            def store(r, carry, arrived=arrived, t=t, half=half):
                value = arrived[t, r].astype(f32)
                for e in range(2):
                    out_ref[0, 2 * r + e, 8 * half : 8 * half + 8, TW * t : TW * t + TW] = value[8 * e : 8 * e + 8]
                return carry

            lax.fori_loop(0, ROW, store, 0, unroll=4)

    most = sent.at[pl.ds(0, SPLIT - 1)]
    remote(most, most, a_send, a_recv.at[0], ahead, worker).wait_send()
    most = quarters.at[pl.ds(0, PAIR - 1)]
    remote(most, most, x_send, x_recv.at[0], ahead, worker).wait_send()
    most = near_in.at[:, pl.ds(0, ROW - 1)]
    remote(most, most, n_send, n_recv.at[0], ahead, worker).wait_send()
    most = far_in.at[:, pl.ds(0, ROW - 1)]
    remote(most, most, f_send, f_recv.at[0], ahead, worker).wait_send()


def shards(raw, pair_list):
    weights, cos, sin = second_tables()
    lag_cos, lag_sin = lag_tables()
    tables = [first_table(), weights, cos, sin, lag_cos, lag_sin, order_tables(), ahead_table()]
    anywhere = pl.BlockSpec(memory_space=pl.ANY)
    vmem = pl.BlockSpec(memory_space=pltpu.VMEM)
    dma = pltpu.SemaphoreType.DMA
    return pl.pallas_call(
        whole_kernel,
        name="whole",
        out_shape=jax.ShapeDtypeStruct((1, 32, 2 * REACH, LAG), f32),
        in_specs=[anywhere, vmem] + [anywhere] * len(tables),
        out_specs=vmem,
        scratch_shapes=[
            pltpu.VMEM(raw.shape, bf16),
            *(pltpu.VMEM(table.shape, table.dtype) for table in tables),
            pltpu.VMEM((SPLIT, 32, 128), bf16),
            pltpu.VMEM((SPLIT, 32, 128), bf16),
            pltpu.VMEM((PAIR, 1024, 128), bf16),
            pltpu.VMEM((PAIR, 1024, 128), bf16),
            pltpu.VMEM((PAIR * 1024, 128), f32),
            pltpu.VMEM((32, 128, 128), f32),
            pltpu.VMEM((NBINS, 128), f32),
            pltpu.VMEM((NBINS, 128), f32),
            pltpu.VMEM((2, NBINS, 128), bf16),
            pltpu.VMEM((CHUNKS, 2, EROWS, 128), bf16),
            pltpu.VMEM((CHUNKS, 2, EROWS, 128), bf16),
            pltpu.VMEM((NBINS, 256), bf16),
            pltpu.VMEM((NBINS, 256), bf16),
            pltpu.VMEM((TCH, ROW, 16, TW), bf16),
            pltpu.VMEM((TCH, 16 * REACH, TW), bf16),
            pltpu.VMEM((TCH, 16 * REACH, TW), bf16),
            pltpu.VMEM((TCH, 16 * ROW, TW), bf16),
            pltpu.VMEM((TCH, ROW, 16, TW), bf16),
            pltpu.VMEM((TCH, ROW, 16, TW), bf16),
            dma((9,)),
            dma,
            dma((4,)),
            dma,
            dma((4,)),
            dma((CHUNKS,)),
            dma((CHUNKS,)),
            dma,
            dma((TCH,)),
            dma,
            dma((TCH,)),
            dma((TCH,)),
            dma((TCH,)),
        ],
        compiler_params=pltpu.CompilerParams(
            collective_id=0, has_side_effects=True, vmem_limit_bytes=VMEM
        ),
    )(raw, pair_list, *(jnp.asarray(table) for table in tables))


def solution(mesh):
    return jax.shard_map(
        shards,
        mesh=mesh,
        in_specs=(P("blk", "pair", None), P()),
        out_specs=P("blk", "pair", None, None),
        check_vma=False,
    )
```

profile of v0, /device:TPU:1, one launch (start us, length us, event | category | flops | bytes accessed | tf_op | source)
XLA Modules:
  0.0 89.4 jit_solution(1093210677132862671)
XLA Ops:
  0.0 1.6 %copy.11.pair_ref = s32[768,2]{1,0:T(8,128)} copy(s32[768,2]{0,1:T(2,128)} %param.11) | data formatting | bytes 12288 | tf_op args[1]
  1.6 85.4 %whole.1 = f32[1,32,16,512]{3,2,1,0:T(8,128)} custom-call(bf16[1,32,16384]{2,1,0:T(8,128)(2,1)} %raw_hbm.1, s32[768,2]{1,0:T(8,128)} %copy.11.pair_ref, bf16[128,128]{1,0:T(8,128)(2,1)} %constant.16.clone.t_hbm, bf16[64,80,192]{2,1,0:T(8,128)(2,1)} %constant.17.clone.w_hbm, f32[64,40,128]{2,1,0:T(8,128)} %constant.18.clone.c_hbm, ...), custom_call_target="tpu_custom_call" | custom-call | tf_op jit(solution)/shard_map/whole/pallas_call | solution.py:394
  87.0 2.3 %copy.13 = f32[1,32,16,512]{3,2,1,0:T(8,128)} copy(f32[1,32,16,512]{3,2,1,0:T(8,128)} %whole.1) | data formatting | bytes 2097152
where the time goes:
time: 89.6 us; the launch traced here: 89.4 us
  Pallas kernels  85.4 us (95%)
  local copies, waits for them, and re-layouts  3.93 us (4%)
    pallas_call x1, Pallas kernels, shards(): pl.pallas_call(whole_kernel, name='whole', out_shape=jax.ShapeDtypeStruct...  85.4 us
    unnamed x2, local copies, waits for them, and re-layouts  3.93 us

commit v1 on v0

--- a/solution.py
+++ b/solution.py
@@ -107,7 +107,10 @@
     return tiles
 
 
-WAVES = ((3, 5), (0, 4), (2, 6), (1, 7))
+WAVES = (1, 7, 4, 2, 6, 3, 5, 0)
+LOOK = 3
+PITCH = 40
+FPITCH = 136
 CHUNKS = 4
 CROWS = NBINS // CHUNKS
 EROWS = CROWS // 8
@@ -118,8 +121,8 @@
 def whole_kernel(
     raw_hbm, pair_ref, t_hbm, w_hbm, c_hbm, s_hbm, lc_hbm, ls_hbm, order_hbm, ahead_hbm, out_ref,
     raw_ref, t_ref, w_ref, c_ref, s_ref, lc_ref, ls_ref, order_ref, ahead_ref,
-    sent, landed, quarters, zs, wide, first, spec_re, spec_im, white, edge_out, edge_in,
-    cross_re, cross_im, near_out, wrap_out, wrap_in, far_out, near_in, far_in,
+    stage, quarters, swapped, sent, landed, wide, first, spec_re, spec_im, white, edge_out, edge_in,
+    cross_re, cross_im, present, near_out, wrap_out, wrap_in, far_out, near_in, far_in,
     load_sem, a_send, a_recv, x_send, x_recv, e_send, e_recv, n_send, n_recv, f_send, f_recv, w_send, w_recv,
 ):
     me, worker = lax.axis_index("blk"), lax.axis_index("pair")
@@ -136,8 +139,7 @@
             )
         )
     ]
-    for load in loads:
-        load.start()
+    loads[0].start()
 
     def remote(source, target, send, recv, blk, pair):
         return pltpu.make_async_remote_copy(
@@ -146,110 +148,140 @@
 
     barrier = pltpu.get_barrier_semaphore()
 
-    def greet(step, carry):
+    def greet(step):
         pl.semaphore_signal(
             barrier, inc=1, device_id=(lax.rem(me + step, SPLIT), worker), device_id_type=MESH
         )
-        return carry
-
-    lax.fori_loop(1, SPLIT, greet, 0)
+
     for step in range(1, PAIR):
         pl.semaphore_signal(
             barrier, inc=1, device_id=(me, lax.rem(worker + step, PAIR)), device_id_type=MESH
         )
-
+    lax.fori_loop(113, SPLIT, lambda step, carry: (greet(step), carry)[1], 0)
     loads[0].wait()
 
-    def spread(index, carry):
-        to_row, half = index // 2, index % 2
-        rows = pl.ds(pl.multiple_of(half * 16, 16), 16)
-        tiles = []
-        for block in range(ROW):
-            at = pl.multiple_of(to_row * 2048 + block * 128, 128)
-            tiles.append(raw_ref[0, rows, pl.ds(at, 128)].astype(f32))
-        tiles = swap_bits(tiles, [(1, 2), (2, 4), (4, 8), (8, 16)])
-        for block in range(ROW):
-            sent[to_row * ROW + block, rows, :] = tiles[block].astype(bf16)
-        return carry
-
-    lax.fori_loop(0, 16, spread, 0)
-
-    lane = lax.broadcasted_iota(jnp.int32, (1, 256), 1)
-    leading = row * ROW + (lane // 2) % ROW
-    trailing = leading + lane // 32 + 1
-    listed = pair_ref[...]
-    found = (listed[:, 0:1] == leading) & (listed[:, 1:2] == trailing)
-    present = jnp.max(jnp.where(found, 1.0, 0.0), axis=0, keepdims=True)
-
+    def spread(to_row, greeting):
+        for half in range(2):
+            for step in range(56 * half + 1, 56 * half + 57):
+                if greeting:
+                    greet(step)
+            rows = pl.ds(16 * half, 16)
+            tiles = []
+            for block in range(ROW):
+                at = pl.multiple_of(to_row * 2048 + block * 128, 128)
+                tiles.append(raw_ref[0, rows, pl.ds(at, 128)].astype(f32))
+            tiles = swap_bits(tiles, [(1, 2), (2, 4), (4, 8), (8, 16)])
+            for block in range(ROW):
+                stage[block, rows, :] = tiles[block].astype(bf16)
+
+    def quarter(to_row):
+        def some(index, carry):
+            parts = []
+            for k in range(2):
+                block = stage[index * 2 + k].astype(f32)
+                tiles = [block[8 * q : 8 * q + 8] for q in range(4)]
+                parts.append(swap_bits(tiles, [(1, 32), (2, 64)]))
+            at = pl.ds(pl.multiple_of(index * 16, 16), 16)
+            for w in range(PAIR):
+                quarters[w, to_row, at, :] = jnp.concatenate([parts[0][w], parts[1][w]], 0).astype(bf16)
+            return carry
+
+        lax.fori_loop(0, 8, some, 0, unroll=4)
+
+    def prepare(wave):
+        to_row = lax.rem(row + WAVES[wave], NROW)
+        spread(to_row, wave == 0)
+        quarter(to_row)
+
+    def swap_workers(wave):
+        to_row = lax.rem(row + WAVES[wave], NROW)
+        for step in range(1, PAIR):
+            there = lax.rem(worker + step, PAIR)
+            remote(
+                quarters.at[there, to_row], swapped.at[worker, to_row], x_send, x_recv.at[wave], me, there
+            ).start()
+        swapped[worker, to_row] = quarters[worker, to_row]
+
+    def issue(wave):
+        to_row = lax.rem(row + WAVES[wave], NROW)
+        part = swapped.at[pl.ds(0, PAIR - 1), 0]
+        remote(part, part, x_send, x_recv.at[wave], me, lax.rem(worker + 1, PAIR)).wait_recv()
+
+        def join(index, carry):
+            at = pl.ds(pl.multiple_of(index * 16, 16), 16)
+            parts = [swapped[w, to_row, at, :].astype(f32) for w in range(PAIR)]
+            for k in range(2):
+                whole = jnp.concatenate([part[8 * k : 8 * k + 8] for part in parts], 0)
+                sent[to_row * ROW + index * 2 + k] = whole.astype(bf16)
+            return carry
+
+        lax.fori_loop(0, 8, join, 0, unroll=4)
+
+        def send(step, carry):
+            shift = (step * 7) % 16
+            chip = lax.rem(place // 2 + shift // 2, 8)
+            core = lax.rem(place % 2 + shift % 2, 2)
+            there = to_row * ROW + chip * 2 + core
+            remote(sent.at[there], landed.at[me], a_send, a_recv.at[wave], there, worker).start()
+            return carry
+
+        lax.fori_loop(1, 16, send, 0)
+        if WAVES[wave]:
+            there = to_row * ROW + place
+            remote(sent.at[there], landed.at[me], a_send, a_recv.at[wave], there, worker).start()
+        else:
+            landed[me] = sent[me]
+
+    prepare(0)
     pl.semaphore_wait(barrier, SPLIT - 1 + PAIR - 1)
-
-    for wave, (one, two) in enumerate(WAVES):
-
-        def send(step, carry, wave=wave, one=one, two=two):
-            to_row = lax.rem(row + one + (two - one) * (step % 2), NROW)
-            shift = ((step // 2) * 7) % 16
-            chip = lax.rem(place // 2 + shift // 2, 8)
-            there = to_row * ROW + chip * 2 + lax.rem(place % 2 + shift % 2, 2)
-            remote(sent.at[there], landed.at[me], a_send, a_recv.at[wave], there, worker).start()
-            return carry
-
-        lax.fori_loop(1 if one == 0 else 0, 32, send, 0)
-    landed[me] = sent[me]
-
-    for wave, (one, two) in enumerate(WAVES):
-        count = 31 if one == 0 else 32
+    swap_workers(0)
+    for wave in range(1, NROW + LOOK):
+        if wave < NROW:
+            prepare(wave)
+            swap_workers(wave)
+        if wave >= LOOK:
+            issue(wave - LOOK)
+        if wave == LOOK:
+            for load in loads[1:]:
+                load.start()
+
+    index = lax.broadcasted_iota(jnp.int32, (256, 768), 0)
+    block, step = index // 16, index % REACH + 1
+    for k, leading in enumerate((row * ROW + block, row * ROW + (block - step + ROW) % ROW)):
+        found = (pair_ref[0:1, :] == leading) & (pair_ref[1:2, :] == leading + step)
+        listed = jnp.max(jnp.where(found, 1.0, 0.0), axis=1, keepdims=True)
+        present[k] = jnp.broadcast_to(listed, (256, 128))
+
+    for load in loads[1:]:
+        load.wait()
+    for wave, distance in enumerate(WAVES):
+        count = 15 if distance == 0 else 16
         remote(
             sent.at[pl.ds(0, count)], landed.at[pl.ds(0, count)], a_send, a_recv.at[wave], ahead, worker
         ).wait_recv()
-        for distance in (one, two):
-            from_row = lax.rem(row + NROW - distance, NROW)
-
-            def quarter(index, carry, from_row=from_row):
-                parts = []
-                for k in range(2):
-                    block = landed[from_row * ROW + index * 2 + k].astype(f32)
-                    tiles = [block[8 * q : 8 * q + 8] for q in range(4)]
-                    parts.append(swap_bits(tiles, [(1, 32), (2, 64)]))
-                at = pl.ds(pl.multiple_of(from_row * 128 + index * 16, 16), 16)
-                for w in range(PAIR):
-                    quarters[w, at, :] = jnp.concatenate([parts[0][w], parts[1][w]], 0).astype(bf16)
-                return carry
-
-            lax.fori_loop(0, 8, quarter, 0, unroll=4)
-            at = pl.ds(pl.multiple_of(from_row * 128, 128), 128)
-            for step in range(1, PAIR):
-                there = lax.rem(worker + step, PAIR)
-                remote(
-                    quarters.at[there, at], zs.at[worker, at], x_send, x_recv.at[wave], me, there
-                ).start()
-            zs[worker, at, :] = quarters[worker, at, :]
-
-    for load in loads[1:]:
-        load.wait()
-    for wave, (one, two) in enumerate(WAVES):
-        part = zs.at[pl.ds(0, PAIR - 1), pl.ds(0, 256)]
-        remote(part, part, x_send, x_recv.at[wave], me, lax.rem(worker + 1, PAIR)).wait_recv()
-        for distance in (one, two):
-            from_row = lax.rem(row + NROW - distance, NROW)
-            at = pl.multiple_of(from_row * 128, 128)
-            for w in range(PAIR):
-                wide[pl.ds(1024 * w + at, 128), :] = zs[w, pl.ds(at, 128), :].astype(f32)
+        from_row = lax.rem(row + NROW - distance, NROW)
+
+        def widen(index, carry, from_row=from_row):
+            source = from_row * ROW + index
+            wide[pl.ds(pl.multiple_of(source * PITCH, 8), 32), :] = landed[source].astype(f32)
+            return carry
+
+        lax.fori_loop(0, ROW, widen, 0, unroll=4)
     table = t_ref[...]
 
     def transform(index, carry):
-        at = (index // 4) * 1024 + (index % 4) * 2
-        pair = [wide[pl.ds(at + k, 128, stride=8), :].astype(bf16) for k in range(2)]
+        pair = [wide[pl.ds(index * 2 + k, 128, stride=PITCH), :].astype(bf16) for k in range(2)]
         got = jnp.dot(table, jnp.concatenate(pair, 1), preferred_element_type=f32)
-        first[index * 2] = got[:, :128]
-        first[index * 2 + 1] = got[:, 128:]
+        for k in range(2):
+            first[index * 2 + k, pl.ds(0, 128)] = got[:, 128 * k : 128 * k + 128]
         return carry
 
     lax.fori_loop(0, 16, transform, 0, unroll=8)
-    flat = first.reshape(32 * 128, 128)
+    flat = first.reshape(32 * FPITCH, 128)
 
     def bands(slot, power):
-        a = flat[pl.ds(slot, 32, stride=128), :]
-        b = flat[pl.ds(slot + HALF, 32, stride=128), :]
+        a = flat[pl.ds(slot, 32, stride=FPITCH), :]
+        b = flat[pl.ds(slot + HALF, 32, stride=FPITCH), :]
         both = jnp.concatenate([a, b], 0)
         high = both.astype(bf16)
         low = (both - high.astype(f32)).astype(bf16)
@@ -269,7 +301,7 @@
         spec_im[at, :] = im
         return power + re * re + im * im
 
-    power = lax.fori_loop(0, HALF, bands, jnp.zeros((BINS, 128), f32), unroll=8)
+    power = lax.fori_loop(0, HALF, bands, jnp.zeros((BINS, 128), f32), unroll=16)
     parity = lax.broadcasted_iota(jnp.int32, (BINS, 128), 0) % 2
     other = jnp.where(parity == 0, pltpu.roll(power, BINS - 1, 0), pltpu.roll(power, 1, 0))
     gain = lax.rsqrt((power + other) / SPLIT + EPSILON)
@@ -320,15 +352,18 @@
         lags = pl.ds(TW * t, TW)
         even = jnp.dot(lc_ref[lags, :], cross_re[...], preferred_element_type=f32)
         odd = jnp.dot(ls_ref[lags, :], cross_im[...], preferred_element_type=f32)
+        near, far = ((half * inv_root).astype(bf16) for half in (even - odd, even + odd))
         near, far = (
-            jnp.where(present > 0.5, half * inv_root, 0.0).astype(bf16)
-            for half in (even - odd, even + odd)
-        )
-        far = lax.dot_general(order_ref[1], far, nt, preferred_element_type=f32).astype(bf16)
+            lax.dot_general(order_ref[k], half, nt, preferred_element_type=f32)
+            for k, half in enumerate((near, far))
+        )
+        near, far = (
+            jnp.where(jnp.concatenate([present[k]] * (TW // 128), 1) > 0.5, half, 0.0).astype(bf16)
+            for k, half in enumerate((near, far))
+        )
         wrap_out[t] = far[: 16 * REACH]
         far_out[t] = far
         remote(wrap_out.at[t], wrap_in.at[t], w_send.at[t], w_recv.at[t], ahead, worker).start()
-        near = lax.dot_general(order_ref[0], near, nt, preferred_element_type=f32).astype(bf16)
         near_out[t] = near.reshape(ROW, 16, TW)
 
         def send_near(step, carry, t=t):
@@ -361,18 +396,19 @@
     for t in range(TCH):
         near_in[t, place] = near_out[t, place]
         far_in[t, place] = far_out[t, pl.ds(pl.multiple_of(place * 16, 16), 16), :]
-    for half, (arrived, send, recv) in enumerate(((near_in, n_send, n_recv), (far_in, f_send, f_recv))):
-        for t in range(TCH):
+    for t in range(TCH):
+        for arrived, send, recv in ((near_in, n_send, n_recv), (far_in, f_send, f_recv)):
             most = arrived.at[t, pl.ds(0, ROW - 1)]
             remote(most, most, send, recv.at[t], ahead, worker).wait_recv()
 
-            def store(r, carry, arrived=arrived, t=t, half=half):
-                value = arrived[t, r].astype(f32)
-                for e in range(2):
-                    out_ref[0, 2 * r + e, 8 * half : 8 * half + 8, TW * t : TW * t + TW] = value[8 * e : 8 * e + 8]
-                return carry
-
-            lax.fori_loop(0, ROW, store, 0, unroll=4)
+        def store(r, carry, t=t):
+            near, far = near_in[t, r].astype(f32), far_in[t, r].astype(f32)
+            for e in range(2):
+                both = jnp.concatenate([near[8 * e : 8 * e + 8], far[8 * e : 8 * e + 8]], 0)
+                out_ref[2 * r + e, :, TW * t : TW * t + TW] = both.astype(bf16)
+            return carry
+
+        lax.fori_loop(0, ROW, store, 0, unroll=4)
 
     most = sent.at[pl.ds(0, SPLIT - 1)]
     remote(most, most, a_send, a_recv.at[0], ahead, worker).wait_send()
@@ -391,21 +427,22 @@
     anywhere = pl.BlockSpec(memory_space=pl.ANY)
     vmem = pl.BlockSpec(memory_space=pltpu.VMEM)
     dma = pltpu.SemaphoreType.DMA
-    return pl.pallas_call(
+    halves = pl.pallas_call(
         whole_kernel,
         name="whole",
-        out_shape=jax.ShapeDtypeStruct((1, 32, 2 * REACH, LAG), f32),
+        out_shape=jax.ShapeDtypeStruct((32, 2 * REACH, LAG), bf16),
         in_specs=[anywhere, vmem] + [anywhere] * len(tables),
         out_specs=vmem,
         scratch_shapes=[
             pltpu.VMEM(raw.shape, bf16),
             *(pltpu.VMEM(table.shape, table.dtype) for table in tables),
+            pltpu.VMEM((ROW, 32, 128), bf16),
+            pltpu.VMEM((PAIR, NROW, 128, 128), bf16),
+            pltpu.VMEM((PAIR, NROW, 128, 128), bf16),
             pltpu.VMEM((SPLIT, 32, 128), bf16),
             pltpu.VMEM((SPLIT, 32, 128), bf16),
-            pltpu.VMEM((PAIR, 1024, 128), bf16),
-            pltpu.VMEM((PAIR, 1024, 128), bf16),
-            pltpu.VMEM((PAIR * 1024, 128), f32),
-            pltpu.VMEM((32, 128, 128), f32),
+            pltpu.VMEM((SPLIT * PITCH, 128), f32),
+            pltpu.VMEM((32, FPITCH, 128), f32),
             pltpu.VMEM((NBINS, 128), f32),
             pltpu.VMEM((NBINS, 128), f32),
             pltpu.VMEM((2, NBINS, 128), bf16),
@@ -413,6 +450,7 @@
             pltpu.VMEM((CHUNKS, 2, EROWS, 128), bf16),
             pltpu.VMEM((NBINS, 256), bf16),
             pltpu.VMEM((NBINS, 256), bf16),
+            pltpu.VMEM((2, 256, 128), f32),
             pltpu.VMEM((TCH, ROW, 16, TW), bf16),
             pltpu.VMEM((TCH, 16 * REACH, TW), bf16),
             pltpu.VMEM((TCH, 16 * REACH, TW), bf16),
@@ -421,9 +459,9 @@
             pltpu.VMEM((TCH, ROW, 16, TW), bf16),
             dma((9,)),
             dma,
-            dma((4,)),
+            dma((len(WAVES),)),
             dma,
-            dma((4,)),
+            dma((len(WAVES),)),
             dma((CHUNKS,)),
             dma((CHUNKS,)),
             dma,
@@ -436,7 +474,8 @@
         compiler_params=pltpu.CompilerParams(
             collective_id=0, has_side_effects=True, vmem_limit_bytes=VMEM
         ),
-    )(raw, pair_list, *(jnp.asarray(table) for table in tables))
+    )(raw, pair_list.T, *(jnp.asarray(table) for table in tables))
+    return halves.astype(f32)[None]
 
 
 def solution(mesh):

time: 89.6 us -> 79.8 us (0.89)
  Pallas kernels: 85.4 us -> 77.4 us
  local copies, waits for them, and re-layouts: 3.93 us -> 0 us
  other arithmetic: 0 us -> 2.15 us
    pallas_call x1, Pallas kernels: 85.4 us -> 77.4 us  [shards(): pl.pallas_call(whole_kernel, name='whole', out_shape=jax.ShapeDtypeStruct...]
    unnamed x2 -> x0, local copies, waits for them, and re-layouts: 3.93 us -> none
    broadcast_in_dim x0 -> x1, other arithmetic: none -> 2.15 us  [shards(): return halves.astype(f32)[None]]
where the time goes in v1:
time: 79.8 us; the launch traced here: 79.5 us
  Pallas kernels  77.4 us (97%)
  other arithmetic  2.15 us (3%)
    pallas_call x1, Pallas kernels, shards(): pl.pallas_call(whole_kernel, name='whole', out_shape=jax.ShapeDtypeStruct...  77.4 us
    broadcast_in_dim x1, other arithmetic, shards(): return halves.astype(f32)[None]  2.15 us

profile of v1, /device:TPU:1, one launch (start us, length us, event | category | flops | bytes accessed | tf_op | source)
XLA Modules:
  0.0 79.5 jit_solution(7278647072552192602)
XLA Ops:
  0.0 77.4 %whole.1 = bf16[32,16,512]{2,1,0:T(8,128)(2,1)} custom-call(bf16[1,32,16384]{2,1,0:T(8,128)(2,1)} %raw_hbm.1, s32[2,768]{1,0:T(2,128)} %bitcast.4, bf16[128,128]{1,0:T(8,128)(2,1)} %constant.16.clone.t_hbm, bf16[64,80,192]{2,1,0:T(8,128)(2,1)} %constant.17.clone.w_hbm, f32[64,40,128]{2,1,0:T(8,128)} %constant.18.clone.c_hbm, ...), custom_call_target="tpu_custom_call" | custom-call | tf_op jit(solution)/shard_map/whole/pallas_call | solution.py:430
  77.4 2.1 %bitcast_convert_fusion = f32[1,32,16,512]{3,2,1,0:T(8,128)} fusion(bf16[32,16,512]{2,1,0:T(8,128)(2,1)} %whole.1), kind=kLoop, calls=%fused_computation | loop fusion | flops 262144 | bytes 1572864 | tf_op jit(solution)/shard_map/broadcast_in_dim | solution.py:478

commit v2 on v1

--- a/solution.py
+++ b/solution.py
@@ -148,23 +148,21 @@
 
     barrier = pltpu.get_barrier_semaphore()
 
-    def greet(step):
+    def greet(step, carry):
         pl.semaphore_signal(
             barrier, inc=1, device_id=(lax.rem(me + step, SPLIT), worker), device_id_type=MESH
         )
+        return carry
 
     for step in range(1, PAIR):
         pl.semaphore_signal(
             barrier, inc=1, device_id=(me, lax.rem(worker + step, PAIR)), device_id_type=MESH
         )
-    lax.fori_loop(113, SPLIT, lambda step, carry: (greet(step), carry)[1], 0)
+    lax.fori_loop(1, SPLIT, greet, 0)
     loads[0].wait()
 
-    def spread(to_row, greeting):
+    def spread(to_row):
         for half in range(2):
-            for step in range(56 * half + 1, 56 * half + 57):
-                if greeting:
-                    greet(step)
             rows = pl.ds(16 * half, 16)
             tiles = []
             for block in range(ROW):
@@ -190,7 +188,7 @@
 
     def prepare(wave):
         to_row = lax.rem(row + WAVES[wave], NROW)
-        spread(to_row, wave == 0)
+        spread(to_row)
         quarter(to_row)
 
     def swap_workers(wave):
@@ -218,7 +216,7 @@
         lax.fori_loop(0, 8, join, 0, unroll=4)
 
         def send(step, carry):
-            shift = (step * 7) % 16
+            shift = (step * 9) % 16
             chip = lax.rem(place // 2 + shift // 2, 8)
             core = lax.rem(place % 2 + shift % 2, 2)
             there = to_row * ROW + chip * 2 + core

time: 79.8 us -> 78.5 us (0.984)
  Pallas kernels: 77.4 us -> 76.2 us
    pallas_call x1, Pallas kernels: 77.4 us -> 76.2 us  [shards(): pl.pallas_call(whole_kernel, name='whole', out_shape=jax.ShapeDtypeStruct...]
where the time goes in v2:
time: 78.5 us; the launch traced here: 78.3 us
  Pallas kernels  76.2 us (97%)
  other arithmetic  2.15 us (3%)
    pallas_call x1, Pallas kernels, shards(): pl.pallas_call(whole_kernel, name='whole', out_shape=jax.ShapeDtypeStruct...  76.2 us
    broadcast_in_dim x1, other arithmetic, shards(): return halves.astype(f32)[None]  2.15 us

profile of v2, /device:TPU:1, one launch (start us, length us, event | category | flops | bytes accessed | tf_op | source)
XLA Modules:
  0.0 78.3 jit_solution(4345639886579526910)
XLA Ops:
  0.0 76.2 %whole.1 = bf16[32,16,512]{2,1,0:T(8,128)(2,1)} custom-call(bf16[1,32,16384]{2,1,0:T(8,128)(2,1)} %raw_hbm.1, s32[2,768]{1,0:T(2,128)} %bitcast.4, bf16[128,128]{1,0:T(8,128)(2,1)} %constant.16.clone.t_hbm, bf16[64,80,192]{2,1,0:T(8,128)(2,1)} %constant.17.clone.w_hbm, f32[64,40,128]{2,1,0:T(8,128)} %constant.18.clone.c_hbm, ...), custom_call_target="tpu_custom_call" | custom-call | tf_op jit(solution)/shard_map/whole/pallas_call | solution.py:428
  76.2 2.1 %bitcast_convert_fusion = f32[1,32,16,512]{3,2,1,0:T(8,128)} fusion(bf16[32,16,512]{2,1,0:T(8,128)(2,1)} %whole.1), kind=kLoop, calls=%fused_computation | loop fusion | flops 262144 | bytes 1572864 | tf_op jit(solution)/shard_map/broadcast_in_dim | solution.py:476

commit v3 on v2

--- a/solution.py
+++ b/solution.py
@@ -341,7 +341,7 @@
                 cross_im[at, columns] = (f * e - a * h).astype(bf16)
             return carry
 
-        lax.fori_loop(0, 8, cross, 0, unroll=2)
+        lax.fori_loop(0, 8, cross, 0, unroll=4)
 
     inv_root = 1.0 / math.sqrt(NBINS)
     offset = lax.broadcasted_iota(jnp.int32, (16, TW), 0) % REACH
@@ -350,19 +350,14 @@
         lags = pl.ds(TW * t, TW)
         even = jnp.dot(lc_ref[lags, :], cross_re[...], preferred_element_type=f32)
         odd = jnp.dot(ls_ref[lags, :], cross_im[...], preferred_element_type=f32)
-        near, far = ((half * inv_root).astype(bf16) for half in (even - odd, even + odd))
-        near, far = (
-            lax.dot_general(order_ref[k], half, nt, preferred_element_type=f32)
-            for k, half in enumerate((near, far))
-        )
-        near, far = (
-            jnp.where(jnp.concatenate([present[k]] * (TW // 128), 1) > 0.5, half, 0.0).astype(bf16)
-            for k, half in enumerate((near, far))
-        )
-        wrap_out[t] = far[: 16 * REACH]
-        far_out[t] = far
-        remote(wrap_out.at[t], wrap_in.at[t], w_send.at[t], w_recv.at[t], ahead, worker).start()
-        near_out[t] = near.reshape(ROW, 16, TW)
+
+        def ordered(k, half):
+            half = (half * inv_root).astype(bf16)
+            half = lax.dot_general(order_ref[k], half, nt, preferred_element_type=f32)
+            listed = jnp.concatenate([present[k]] * (TW // 128), 1) > 0.5
+            return jnp.where(listed, half, 0.0).astype(bf16)
+
+        near_out[t] = ordered(0, even - odd).reshape(ROW, 16, TW)
 
         def send_near(step, carry, t=t):
             to = lax.rem(place + (step * 7) % 16, ROW)
@@ -372,6 +367,10 @@
             return carry
 
         lax.fori_loop(1, ROW, send_near, 0)
+        far = ordered(1, even + odd)
+        wrap_out[t] = far[: 16 * REACH]
+        far_out[t] = far
+        remote(wrap_out.at[t], wrap_in.at[t], w_send.at[t], w_recv.at[t], ahead, worker).start()
 
     for t in range(TCH):
         remote(wrap_out.at[t], wrap_in.at[t], w_send.at[t], w_recv.at[t], ahead, worker).wait()

time: 78.5 us -> 77.8 us (level)
  no operation moved by 1% of the time
where the time goes in v3:
time: 77.8 us; the launch traced here: 77.6 us
  Pallas kernels  75.5 us (97%)
  other arithmetic  2.15 us (3%)
    pallas_call x1, Pallas kernels, shards(): pl.pallas_call(whole_kernel, name='whole', out_shape=jax.ShapeDtypeStruct...  75.5 us
    broadcast_in_dim x1, other arithmetic, shards(): return halves.astype(f32)[None]  2.15 us

profile of v3, /device:TPU:1, one launch (start us, length us, event | category | flops | bytes accessed | tf_op | source)
XLA Modules:
  0.0 77.6 jit_solution(13441649755867967736)
XLA Ops:
  0.0 75.5 %whole.1 = bf16[32,16,512]{2,1,0:T(8,128)(2,1)} custom-call(bf16[1,32,16384]{2,1,0:T(8,128)(2,1)} %raw_hbm.1, s32[2,768]{1,0:T(2,128)} %bitcast.4, bf16[128,128]{1,0:T(8,128)(2,1)} %constant.16.clone.t_hbm, bf16[64,80,192]{2,1,0:T(8,128)(2,1)} %constant.17.clone.w_hbm, f32[64,40,128]{2,1,0:T(8,128)} %constant.18.clone.c_hbm, ...), custom_call_target="tpu_custom_call" | custom-call | tf_op jit(solution)/shard_map/whole/pallas_call | solution.py:427
  75.5 2.1 %bitcast_convert_fusion = f32[1,32,16,512]{3,2,1,0:T(8,128)} fusion(bf16[32,16,512]{2,1,0:T(8,128)(2,1)} %whole.1), kind=kLoop, calls=%fused_computation | loop fusion | flops 262144 | bytes 1572864 | tf_op jit(solution)/shard_map/broadcast_in_dim | solution.py:475
